TPU v7x, 512 devices: a whole 4x4x16 slice. The times are simulated.
512 devices in a mesh: dp: 16 (over y, z_hi, core), expert: 8 (over z_lo), mp: 4 (over x).
Axes of the slice: x: 4, y: 4, z: 16 (z_hi: 2, z_lo: 8; z = z_hi * 8 + z_lo), core: 2. Of those that a mesh axis runs over, the one named last changes fastest.
Arguments:
- expert_ids: int32 [2048, 2], P('dp'), may hold values from 0 to 7, all different within a row; in each aligned block of 128 rows (0 to 127, 128 to 255, ...) at most 48 rows name the same one
- gate_weights: float32 [2048, 2], P('dp'), may hold values from 0.1 to 1
- hidden: bfloat16 [8, 768, 8192], P('expert', 'mp', 'dp'), may hold values from -6 to 6
- down_weight: bfloat16 [8, 8192, 6144], P('expert', 'dp', 'mp'), may hold values from -0.0625 to 0.0625
- cotangent: bfloat16 [2048, 6144], P('dp', 'mp'), may hold values from -1.5 to 1.5
Outputs:
- mixed: bfloat16 [2048, 6144], P('dp', 'mp')
- gate_grad: float32 [2048, 2], P('dp')
- hidden_grad: bfloat16 [8, 768, 8192], P('expert', 'mp', 'dp')
- weight_grad: bfloat16 [8, 8192, 6144], P('expert', 'dp', 'mp')
Inputs may be any that keep to these rules, and one draw needn't show every extreme that they name: `expert_ids`: each row names two different experts. Within the 128 rows of one index of dp, no expert is named more than 48 times, a bound that some block reaches.
All inputs are finite; a program needn't handle non-finite values.
Results may differ from a plain program's by a relative error of at most 0.02.
Values may be sent and summed in bfloat16 or wider, within the bound.
A program may use at most 64 MiB of HBM per device.

v0:
```python
import jax
import jax.numpy as jnp
from jax import lax
from jax.sharding import PartitionSpec as P


def body(expert_ids, gate_weights, hidden, down_weight, cotangent):
    experts_all = lax.axis_size("expert")
    slot_count = hidden.shape[1] * lax.axis_size("mp")
    capacity = slot_count // lax.axis_size("dp")
    tok_rows = expert_ids.shape[0]
    own_expert = lax.axis_index("expert")
    flat_ids = expert_ids.reshape(tok_rows * 2)
    onehot = (flat_ids[:, None] == jnp.arange(experts_all, dtype=jnp.int32)[None, :]).astype(
        jnp.int32
    )
    before = jnp.cumsum(onehot, axis=0) - onehot
    position = jnp.sum(before * onehot, axis=1).reshape(tok_rows, 2)
    weight = down_weight[0]
    gathered = lax.all_gather(hidden[0], "mp", axis=0, tiled=True)
    piece = gathered
    out_rows = lax.psum_scatter(
        jnp.dot(piece, weight, preferred_element_type=jnp.float32).astype(jnp.bfloat16),
        "dp",
        scatter_dimension=0,
        tiled=True,
    )
    cot_f32 = cotangent.astype(jnp.float32)
    slot_range = jnp.arange(capacity, dtype=jnp.int32)

    def select_own(column):
        same_expert = expert_ids[:, column : column + 1] == own_expert
        same_slot = position[:, column : column + 1] == slot_range[None, :]
        return jnp.logical_and(same_expert, same_slot).astype(jnp.bfloat16)

    first_sel = select_own(0)
    second_sel = select_own(1)
    first_scaled = (gate_weights[:, 0:1] * cot_f32).astype(jnp.bfloat16)
    second_scaled = (gate_weights[:, 1:2] * cot_f32).astype(jnp.bfloat16)
    contract_rows = (((0,), (0,)), ((), ()))
    slot_cot = (
        lax.dot_general(first_sel, first_scaled, contract_rows, preferred_element_type=jnp.float32)
        + lax.dot_general(
            second_sel, second_scaled, contract_rows, preferred_element_type=jnp.float32
        )
    ).astype(jnp.bfloat16)
    all_cot = lax.all_gather(slot_cot, "dp", axis=0, tiled=True)
    piece = all_cot
    hidden_grad = lax.psum_scatter(
        lax.dot_general(
            piece, weight, (((1,), (1,)), ((), ())), preferred_element_type=jnp.float32
        ).astype(jnp.bfloat16),
        "mp",
        scatter_dimension=0,
        tiled=True,
    )[None]
    weight_grad = lax.dot_general(
        gathered, all_cot, contract_rows, preferred_element_type=jnp.float32
    ).astype(jnp.bfloat16)[None]
    first_rows = jnp.dot(first_sel, out_rows, preferred_element_type=jnp.float32)
    second_rows = jnp.dot(second_sel, out_rows, preferred_element_type=jnp.float32)
    token_part = gate_weights[:, 0:1] * first_rows + gate_weights[:, 1:2] * second_rows
    gate_part = jnp.stack(
        [jnp.sum(first_rows * cot_f32, axis=1), jnp.sum(second_rows * cot_f32, axis=1)], axis=1
    )
    mixed = lax.psum(token_part.astype(jnp.bfloat16), "expert")
    gate_grad = lax.psum(gate_part, ("expert", "mp"))
    return (mixed, gate_grad, hidden_grad, weight_grad)


def solution(mesh):
    in_specs = (
        P("dp", None),
        P("dp", None),
        P("expert", "mp", "dp"),
        P("expert", "dp", "mp"),
        P("dp", "mp"),
    )
    out_specs = (P("dp", "mp"), P("dp", None), P("expert", "mp", "dp"), P("expert", "dp", "mp"))
    return jax.shard_map(body, mesh=mesh, in_specs=in_specs, out_specs=out_specs, check_vma=False)
```

profile of v0, /device:TPU:6, one launch (start us, length us, event | category | flops | bytes accessed | tf_op | source)
XLA Modules:
  0.0 397.0 jit_solution(8035061895493500758)
XLA Ops:
  7.2 0.0 copy-start
  7.2 0.0 reduce-scatter.3.cloned.1.call-start
  7.2 16.3 %all-gather = bf16[1,768,512]{2,1,0:T(8,128)(2,1)S(1)} all-gather(bf16[1,192,512]{2,1,0:T(8,128)(2,1)} %param.7), channel_id=2, replica_groups=mesh['dp'=16,'expert'=8,'mp'=4] {'mp'}, dimensions={1}, use_global_device_ids=true | all-gather | bytes 983040 | tf_op jit(solution)/shard_map/all_gather | solution.py:20
  23.6 0.0 copy-start.2
  23.6 0.9 copy-done.2
  24.5 0.0 copy-done
  24.5 2.8 convolution_convert_fusion
  27.2 0.0 copy-start.3
  27.2 0.0 copy-start.4
  27.2 0.0 copy-start.1
  27.2 0.0 reduce-scatter.3.cloned.1.call-update
  27.3 0.0 all-gather.3.cloned.1.call-start
  27.3 0.6 copy-done.3
  27.9 0.1 copy.13
  28.0 0.1 eq.71
  28.2 0.1 eq.67
  28.3 0.6 reduce-window.6
  28.9 0.2 slice_reduce_fusion.2
  29.2 0.1 fusion.36
  29.3 0.1 reshape.29
  29.4 0.2 slice_reduce_fusion.1
  29.6 0.0 copy-done.4
  29.6 0.0 copy-done.1
  29.6 0.3 fusion.15
  30.0 1.0 fusion.1
  31.0 0.0 all-gather.3.cloned.1.call-update
  31.0 0.0 all-reduce.2.cloned.1.call-start
  31.0 124.8 %reduce-scatter.3.cloned.1.call-done = bf16[48,1536]{1,0:T(8,128)(2,1)} async-done(((bf16[768,1536]{1,0:T(8,128)(2,1)}), bf16[48,1536]{1,0:T(8,128)(2,1)}) %reduce-scatter.3.cloned.1.call-update) | async-done | bytes 147472 | tf_op jit(solution)/shard_map/reduce_scatter | solution.py:22
  155.8 1.2 fusion.25
  157.0 2.1 fusion.8
  159.1 0.0 all-reduce.2.cloned.1.call-update
  159.1 0.0 reduce-scatter.5.cloned.1.call-start
  159.2 87.3 %all-gather.3.cloned.1.call-done = bf16[768,1536]{1,0:T(8,128)(2,1)} async-done(((bf16[48,1536]{1,0:T(8,128)(2,1)}), bf16[768,1536]{1,0:T(8,128)(2,1)}) %all-gather.3.cloned.1.call-update) | async-done | bytes 2359312 | tf_op jit(solution)/shard_map/all_gather | solution.py:47
  246.5 4.0 %fusion.5 = bf16[768,512]{1,0:T(8,128)(2,1)} fusion(bf16[768,1536]{1,0:T(8,128)(2,1)} %all-gather.3.cloned.1.call-done, bf16[1,512,1536]{2,1,0:T(8,128)(2,1)S(1)} %copy-done), kind=kOutput, calls=%fused_computation.8 | convolution fusion | flops 1208352768 | bytes 4718592 | tf_op jit(solution)/shard_map/dot_general | solution.py:50
  250.5 0.0 reduce-scatter.5.cloned.1.call-update
  250.5 104.8 %psum.15 = f32[128,2]{0,1:T(2,128)} all-reduce(f32[128,2]{0,1:T(2,128)S(1)} %pad_maximum_fusion), channel_id=1, replica_groups=mesh['dp'=16,'expert'=8,'mp'=4] {'expert','mp'}, use_global_device_ids=true, to_apply=%region_7.8 | all-reduce | flops 256 | bytes 2048 | tf_op jit(solution)/shard_map/psum | solution.py:67
  355.3 3.3 fusion
  358.6 1.6 copy.15
  360.2 3.1 all-reduce.2.cloned.1.call-done
  363.3 25.4 %reduce-scatter.5.cloned.1.call-done = bf16[192,512]{1,0:T(8,128)(2,1)} async-done(((bf16[768,512]{1,0:T(8,128)(2,1)}), bf16[192,512]{1,0:T(8,128)(2,1)}) %reduce-scatter.5.cloned.1.call-update) | async-done | bytes 196624 | tf_op jit(solution)/shard_map/reduce_scatter | solution.py:49
  388.7 1.8 copy.17
  (6 shorter events, 0.1 us)
Async XLA Ops:
  7.2 17.3 %copy-start = (bf16[1,512,1536]{2,1,0:T(8,128)(2,1)S(1)}, bf16[1,512,1536]{2,1,0:T(8,128)(2,1)}, u32[]{:S(2)}) copy-start(bf16[1,512,1536]{2,1,0:T(8,128)(2,1)} %param.8) | copy-start | bytes 4718596
  7.2 148.6 %reduce-scatter.3.cloned.1.call-start = ((), (), s32[]{:S(2)}) async-start(), calls=%async_computation.2 | async-start | bytes 2506752 | tf_op jit(solution)/shard_map/reduce_scatter | solution.py:22
  23.6 0.9 copy-start.2
  27.2 0.7 copy-start.3
  27.2 2.4 copy-start.4
  27.2 2.4 copy-start.1
  27.3 219.3 %all-gather.3.cloned.1.call-start = ((), (), s32[]{:S(2)}) async-start(), calls=%async_computation.4 | async-start | bytes 2506752 | tf_op jit(solution)/shard_map/all_gather | solution.py:47
  31.0 332.3 %all-reduce.2.cloned.1.call-start = ((), (), s32[]{:S(2)}) async-start(), calls=%async_computation.3 | async-start | bytes 786432 | tf_op jit(solution)/shard_map/psum | solution.py:66
  159.1 229.6 %reduce-scatter.5.cloned.1.call-start = ((), (), s32[]{:S(2)}) async-start(), calls=%async_computation.5 | async-start | bytes 983040 | tf_op jit(solution)/shard_map/reduce_scatter | solution.py:49
Sparse Core Ops, SparseCore 0:
  27.4 128.3 reduce-scatter.2
  159.7 86.8 all-gather.2
  250.0 113.2 all-reduce.1
  366.8 21.8 reduce-scatter.4
where the time goes:
time: 399 us; the launch traced here: 397 us
  waiting for transfers between devices  241 us (60%)
  blocking collectives  121 us (30%)
  matrix products  14.6 us (4%)
  between operations  13.9 us (3%)
  local copies, waits for them, and re-layouts  5.76 us (1%)
    reduce_scatter x1, waiting for transfers between devices, body(): lax.psum_scatter(jnp.dot(piece, weight, preferred_element_type=jnp.float3...  125 us
    psum x1, blocking collectives, body(): gate_grad = lax.psum(gate_part, ('expert', 'mp'))  105 us
    all_gather x1, waiting for transfers between devices, body(): all_cot = lax.all_gather(slot_cot, 'dp', axis=0, tiled=True)  87.3 us
    reduce_scatter x1, waiting for transfers between devices, body(): lax.psum_scatter(lax.dot_general(piece, weight, (((1,), (1,)), ((), ())),...  25.4 us
    all_gather x1, blocking collectives, body(): gathered = lax.all_gather(hidden[0], 'mp', axis=0, tiled=True)  16.3 us
  transfers between devices with their start and end apart: 4, of which 4 were waited for; matrix products, arithmetic and copies ran while one was open for 4% of the time, Pallas kernels for 0%

commit v1 on v0

v1 whole, which is shorter than its diff:
```python
import jax
import jax.numpy as jnp
from jax import lax
from jax.experimental import pallas as pl
from jax.experimental.pallas import tpu as pltpu
from jax.sharding import PartitionSpec as P

MESH = pl.DeviceIdType.MESH
F32 = jnp.float32
BF16 = jnp.bfloat16
NT = (((1,), (1,)), ((), ()))
TN = (((0,), (0,)), ((), ()))

NX, NY, NE = 4, 4, 8
CAP, ROWS, DEPTH, COLS, TOKS = 48, 192, 512, 1536, 128
GROUPS = 3
WIDE = COLS // GROUPS
LANES = 128
CHUNKS = COLS // LANES
PER_GROUP = WIDE // LANES
STEPS = CHUNKS + NE - 1


def kernel(
    ids_ref, gates_ref, hidden_ref, weight_ref, cot_ref,
    mixed_ref, gate_ref, hgrad_ref, wgrad_ref,
    hid_all, slot_all, cot_sel, parts, core_rx, core_sum, y_rx, z_own, z_tx, z_rx,
    tok, up_tx, up_rx, down_tx, down_rx, hg_tx, hg_rx, gate_tx, gate_sum, gate_xrx, gate_erx, gate_acc,
    hid_sem, slot_z_sem, slot_y_sem, slot_c_sem, core_sem, y_sem, z_sem, up_sem, down_sem, hg_sem, gx_sem, ge_sem,
):
    dp = lax.axis_index("dp")
    ex = lax.axis_index("expert")
    mx = lax.axis_index("mp")
    core = dp % 2
    half = (dp // 2) % 2
    row = dp // 4

    def dp_of(y, h, c):
        return (y * 2 + h) * 2 + c

    def x_peer(d):
        return {"mp": (mx + d) % NX}

    def y_peer(d):
        return {"dp": dp_of((row + d) % NY, half, core)}

    def e_peer(d):
        return {"expert": (ex + d) % NE}

    core_peer = {"dp": dp_of(row, half, 1 - core)}
    half_peer = {"dp": dp_of(row, 1 - half, core)}

    def remote(src, dst, sems, index, peer):
        return pltpu.make_async_remote_copy(
            src_ref=src,
            dst_ref=dst,
            send_sem=sems.at[(0, *index)],
            recv_sem=sems.at[(1, *index)],
            device_id=peer,
            device_id_type=MESH,
        )

    barrier = pltpu.get_barrier_semaphore()
    peers = [x_peer(d) for d in range(1, NX)] + [y_peer(d) for d in range(1, NY)]
    peers += [e_peer(d) for d in range(1, NE)] + [core_peer, half_peer]
    for peer in peers:
        pl.semaphore_signal(barrier, inc=1, device_id=peer, device_id_type=MESH)

    hit0 = (ids_ref[0:1, :] == ex).astype(F32)
    hit1 = (ids_ref[1:2, :] == ex).astype(F32)
    hits = hit0 + hit1
    gate_of = hit0 * gates_ref[0:1, :] + hit1 * gates_ref[1:2, :]
    earlier = lax.broadcasted_iota(jnp.int32, (TOKS, TOKS), 0) < lax.broadcasted_iota(
        jnp.int32, (TOKS, TOKS), 1
    )
    place = jnp.dot(
        jnp.broadcast_to(hits, (16, TOKS)).astype(BF16),
        earlier.astype(F32).astype(BF16),
        preferred_element_type=F32,
    )[0:1, :]
    slot = lax.broadcasted_iota(jnp.int32, (CAP, TOKS), 0).astype(F32)
    sel = jnp.where(slot == place, jnp.broadcast_to(hits, (CAP, TOKS)), 0.0)
    slot_gate = jnp.sum(sel * gate_of, axis=1, keepdims=True)
    sel16 = sel.astype(BF16)
    picked = jnp.dot(sel16, cot_ref[...], preferred_element_type=F32)
    cot_sel[...] = picked
    slot_all[dp] = (slot_gate * picked).astype(BF16)
    hid_all[mx] = hidden_ref[...]
    gate_acc[...] = jnp.zeros_like(gate_acc)

    pl.semaphore_wait(barrier, len(peers))

    hid_copies = [
        remote(hidden_ref, hid_all.at[mx], hid_sem, (d - 1,), x_peer(d)) for d in (1, 3, 2)
    ]
    for copy in hid_copies:
        copy.start()

    def slot_y(side, block):
        return [
            remote(slot_all.at[block], slot_all.at[block], slot_y_sem, (side, d - 1), y_peer(d))
            for d in (1, 3, 2)
        ]

    def slot_core(index, block):
        return remote(slot_all.at[block], slot_all.at[block], slot_c_sem, (index,), core_peer)

    other_block = dp_of(row, 1 - half, core)
    slot_z = remote(slot_all.at[dp], slot_all.at[dp], slot_z_sem, (0,), half_peer)
    slot_z.start()
    own_y = slot_y(0, dp)
    for copy in own_y:
        copy.start()
    core_copies = [slot_core(0, dp)]
    core_copies[0].start()

    for copy in hid_copies:
        copy.wait_recv()
    rows_all = hid_all[...].reshape(NX * ROWS, DEPTH)
    to_core = []
    for g in range(GROUPS):
        product = jnp.dot(
            rows_all, weight_ref[:, g * WIDE : (g + 1) * WIDE], preferred_element_type=F32
        ).astype(BF16)
        product = product.reshape(NY, 2, 2, CAP, WIDE)
        for c in range(2):
            parts[g, c] = product[:, :, c]
        copy = remote(parts.at[g, 1 - core], core_rx.at[g], core_sem, (g,), core_peer)
        copy.start()
        to_core.append(copy)

    to_y = []
    for g in range(GROUPS):
        to_core[g].wait_recv()
        core_sum[g] = (parts[g, core].astype(F32) + core_rx[g].astype(F32)).astype(BF16)
        group = []
        for d in (2, 1, 3):
            copy = remote(
                core_sum.at[g, (row + d) % NY], y_rx.at[g, d - 1], y_sem, (g, d - 1), y_peer(d)
            )
            copy.start()
            group.append(copy)
        to_y.append(group)

    for n, copy in enumerate(own_y):
        copy.wait_recv()
        d = (1, 3, 2)[n]
        onward = slot_core(1 + n, dp_of((row - d + NY) % NY, half, core))
        onward.start()
        core_copies.append(onward)
    slot_z.wait_recv()
    other_y = slot_y(1, other_block)
    for copy in other_y:
        copy.start()
    onward = slot_core(4, other_block)
    onward.start()
    core_copies.append(onward)

    to_z = []
    for g in range(GROUPS):
        for copy in to_y[g]:
            copy.wait_recv()
        mine = core_sum[g, row].astype(F32)
        for d in range(1, NY):
            mine = mine + y_rx[g, d - 1].astype(F32)
        z_own[g] = mine
        z_tx[g] = z_own[g, 1 - half].astype(BF16)
        copy = remote(z_tx.at[g], z_rx.at[g], z_sem, (g,), half_peer)
        copy.start()
        to_z.append(copy)

    for n, copy in enumerate(other_y):
        copy.wait_recv()
        d = (1, 3, 2)[n]
        onward = slot_core(5 + n, dp_of((row - d + NY) % NY, 1 - half, core))
        onward.start()
        core_copies.append(onward)
    for copy in core_copies:
        copy.wait_recv()

    slots = slot_all[...].reshape(NX * ROWS, COLS)
    hg_tx[...] = (
        lax.dot_general(slots, weight_ref[...], NT, preferred_element_type=F32)
        .astype(BF16)
        .reshape(NX, ROWS, DEPTH)
    )
    hg_copies = [
        remote(hg_tx.at[(mx + d) % NX], hg_rx.at[d - 1], hg_sem, (d - 1,), x_peer(d))
        for d in (2, 1, 3)
    ]
    for copy in hg_copies:
        copy.start()
    rows_t = hid_all[...].reshape(NX * ROWS, DEPTH).T
    for g in range(GROUPS):
        wgrad_ref[:, g * WIDE : (g + 1) * WIDE] = jnp.dot(
            rows_t,
            slot_all[:, :, g * WIDE : (g + 1) * WIDE].reshape(NX * ROWS, WIDE),
            preferred_element_type=F32,
        ).astype(BF16)

    sel_t = sel.T.astype(BF16)

    def take_group(g):
        remote(z_tx.at[g], z_rx.at[g], z_sem, (g,), half_peer).wait_recv()
        out = (z_own[g, half] + z_rx[g].astype(F32)).astype(BF16).astype(F32)
        for n in range(GROUPS):

            @pl.when(g == n)
            def _():
                dots = out * cot_sel[:, n * WIDE : (n + 1) * WIDE]
                gate_acc[...] += jnp.sum(dots, axis=1, keepdims=True)

        weighted = jnp.dot(
            sel_t, (slot_gate * out).astype(BF16), preferred_element_type=F32
        ).astype(BF16)
        for n in range(PER_GROUP):
            tok[g * PER_GROUP + n] = weighted[:, n * LANES : (n + 1) * LANES]

    up_peer, down_peer = e_peer(1), e_peer(NE - 1)

    def up_copy(q):
        return remote(up_tx.at[q], up_rx.at[q], up_sem, (q,), up_peer)

    def down_copy(q):
        return remote(down_tx.at[q], down_rx.at[q], down_sem, (q,), down_peer)

    gate_x = [remote(gate_tx, gate_xrx.at[d - 1], gx_sem, (d - 1,), x_peer(d)) for d in (2, 1, 3)]
    gate_e = [
        remote(gate_sum, gate_erx.at[d - 1], ge_sem, (d - 1,), e_peer(d)) for d in range(1, NE)
    ]

    def step(s, carry):
        @pl.when(jnp.logical_and(s % PER_GROUP == 0, s < CHUNKS))
        def _():
            take_group(s // PER_GROUP)

        @pl.when(s == CHUNKS - 1)
        def _():
            per_token = jnp.sum(sel * gate_acc[:, 0:1], axis=0, keepdims=True)
            gate_tx[...] = jnp.zeros_like(gate_tx)
            gate_tx[0:1, :] = per_token * hit0
            gate_tx[1:2, :] = per_token * hit1
            for copy in gate_x:
                copy.start()

        @pl.when(s == CHUNKS + 2)
        def _():
            for copy in gate_x:
                copy.wait_recv()
            gate_sum[...] = gate_tx[...] + gate_xrx[0] + gate_xrx[1] + gate_xrx[2]
            for copy in gate_e:
                copy.start()

        q = s - ex

        @pl.when(jnp.logical_and(q >= 0, q < CHUNKS))
        def _():
            @pl.when(ex == 0)
            def _():
                up_tx[q] = tok[q]

            @pl.when(ex > 0)
            def _():
                up_copy(q).wait_recv()
                up_tx[q] = (tok[q].astype(F32) + up_rx[q].astype(F32)).astype(BF16)

            @pl.when(ex < NE - 1)
            def _():
                up_copy(q).start()

        r = s - (NE - 1 - ex)

        @pl.when(jnp.logical_and(r >= 0, r < CHUNKS))
        def _():
            @pl.when(ex == NE - 1)
            def _():
                down_tx[r] = tok[r]

            @pl.when(ex < NE - 1)
            def _():
                down_copy(r).wait_recv()
                down_tx[r] = (tok[r].astype(F32) + down_rx[r].astype(F32)).astype(BF16)

            @pl.when(ex > 0)
            def _():
                down_copy(r).start()

        return carry

    lax.fori_loop(0, STEPS, step, 0)

    for q in range(CHUNKS):
        columns = slice(q * LANES, (q + 1) * LANES)

        @pl.when(ex < NE - 1)
        def _():
            mixed_ref[:, columns] = (up_tx[q].astype(F32) + down_rx[q].astype(F32)).astype(BF16)

        @pl.when(ex == NE - 1)
        def _():
            mixed_ref[:, columns] = up_tx[q]

    for copy in hg_copies:
        copy.wait_recv()
    total = hg_tx[mx].astype(F32)
    for d in range(1, NX):
        total = total + hg_rx[d - 1].astype(F32)
    hgrad_ref[...] = total.astype(BF16)

    for copy in gate_e:
        copy.wait_recv()
    gates = gate_sum[...]
    for d in range(1, NE):
        gates = gates + gate_erx[d - 1]
    gate_ref[...] = gates

    for copy in [*hid_copies, slot_z, *own_y, *other_y, *core_copies, *to_core, *to_z]:
        copy.wait_send()
    for group in to_y:
        for copy in group:
            copy.wait_send()
    for copy in [*hg_copies, *gate_x, *gate_e]:
        copy.wait_send()

    def drain(q, carry):
        @pl.when(ex < NE - 1)
        def _():
            up_copy(q).wait_send()

        @pl.when(ex > 0)
        def _():
            down_copy(q).wait_send()

        return carry

    lax.fori_loop(0, CHUNKS, drain, 0)


def body(expert_ids, gate_weights, hidden, down_weight, cotangent):
    vmem = pl.BlockSpec(memory_space=pltpu.VMEM)
    dma = pltpu.SemaphoreType.DMA
    mixed, gates, hgrad, wgrad = pl.pallas_call(
        kernel,
        name="layer",
        out_shape=(
            jax.ShapeDtypeStruct((TOKS, COLS), BF16),
            jax.ShapeDtypeStruct((8, TOKS), F32),
            jax.ShapeDtypeStruct((ROWS, DEPTH), BF16),
            jax.ShapeDtypeStruct((DEPTH, COLS), BF16),
        ),
        in_specs=[vmem] * 5,
        out_specs=(vmem,) * 4,
        scratch_shapes=[
            pltpu.VMEM((NX, ROWS, DEPTH), BF16),
            pltpu.VMEM((16, CAP, COLS), BF16),
            pltpu.VMEM((CAP, COLS), F32),
            pltpu.VMEM((GROUPS, 2, NY, 2, CAP, WIDE), BF16),
            pltpu.VMEM((GROUPS, NY, 2, CAP, WIDE), BF16),
            pltpu.VMEM((GROUPS, NY, 2, CAP, WIDE), BF16),
            pltpu.VMEM((GROUPS, NY - 1, 2, CAP, WIDE), BF16),
            pltpu.VMEM((GROUPS, 2, CAP, WIDE), F32),
            pltpu.VMEM((GROUPS, CAP, WIDE), BF16),
            pltpu.VMEM((GROUPS, CAP, WIDE), BF16),
            pltpu.VMEM((CHUNKS, TOKS, LANES), BF16),
            pltpu.VMEM((CHUNKS, TOKS, LANES), BF16),
            pltpu.VMEM((CHUNKS, TOKS, LANES), BF16),
            pltpu.VMEM((CHUNKS, TOKS, LANES), BF16),
            pltpu.VMEM((CHUNKS, TOKS, LANES), BF16),
            pltpu.VMEM((NX, ROWS, DEPTH), BF16),
            pltpu.VMEM((NX - 1, ROWS, DEPTH), BF16),
            pltpu.VMEM((8, TOKS), F32),
            pltpu.VMEM((8, TOKS), F32),
            pltpu.VMEM((NX - 1, 8, TOKS), F32),
            pltpu.VMEM((NE - 1, 8, TOKS), F32),
            pltpu.VMEM((CAP, TOKS), F32),
            dma((2, NX - 1)),
            dma((2, 1)),
            dma((2, 2, NY - 1)),
            dma((2, 8)),
            dma((2, GROUPS)),
            dma((2, GROUPS, NY - 1)),
            dma((2, GROUPS)),
            dma((2, CHUNKS)),
            dma((2, CHUNKS)),
            dma((2, NX - 1)),
            dma((2, NX - 1)),
            dma((2, NE - 1)),
        ],
        compiler_params=pltpu.CompilerParams(
            collective_id=0, has_side_effects=True, vmem_limit_bytes=50 * 2**20
        ),
    )(expert_ids.T, gate_weights.T, hidden[0], down_weight[0], cotangent)
    return mixed, gates[0:2].T, hgrad[None], wgrad[None]


def solution(mesh):
    in_specs = (
        P("dp", None),
        P("dp", None),
        P("expert", "mp", "dp"),
        P("expert", "dp", "mp"),
        P("dp", "mp"),
    )
    out_specs = (P("dp", "mp"), P("dp", None), P("expert", "mp", "dp"), P("expert", "dp", "mp"))
    return jax.shard_map(body, mesh=mesh, in_specs=in_specs, out_specs=out_specs, check_vma=False)
```

time: 399 us -> 118 us (0.30)
  waiting for transfers between devices: 241 us -> 0 us
  blocking collectives: 121 us -> 0 us
  Pallas kernels: 0 us -> 110 us
  matrix products: 14.6 us -> 0 us
  between operations: 13.9 us -> 0.65 us
    reduce_scatter x2 -> x0, waiting for transfers between devices: 150 us -> none  [the longest x1 125 us: body(): lax.psum_scatter(jnp.dot(piece, weight, preferred_element_type=jnp.float3...]
    pallas_call x0 -> x1, Pallas kernels: none -> 110 us  [body(): pl.pallas_call(kernel, name='layer', out_shape=(jax.ShapeDtypeStruct((TOK...]
    psum x1 -> x0, blocking collectives: 105 us -> none  [body(): gate_grad = lax.psum(gate_part, ('expert', 'mp'))]
    all_gather x1 -> x0, waiting for transfers between devices: 87.3 us -> none  [body(): all_cot = lax.all_gather(slot_cot, 'dp', axis=0, tiled=True)]
    all_gather x1 -> x0, blocking collectives: 16.3 us -> none  [body(): gathered = lax.all_gather(hidden[0], 'mp', axis=0, tiled=True)]
    dot_general x7 -> x0, matrix products: 14.6 us -> none  [the longest x1 3.97 us: body(): lax.dot_general(piece, weight, (((1,), (1,)), ((), ())), preferred_elemen...]
  transfers between devices with their start and end apart: 4 -> 0, of which waited for: 4 -> 0; matrix products, arithmetic and copies ran while one was open for 4% -> 0% of each run, Pallas kernels for 0% -> 0%
where the time goes in v1:
time: 118 us; the launch traced here: 117 us
  Pallas kernels  110 us (93%)
  local copies, waits for them, and re-layouts  6.4 us (5%)
    pallas_call x1, Pallas kernels, body(): pl.pallas_call(kernel, name='layer', out_shape=(jax.ShapeDtypeStruct((TOK...  110 us
    unnamed x11, local copies, waits for them, and re-layouts  5.84 us

profile of v1, /device:TPU:6, one launch (start us, length us, event | category | flops | bytes accessed | tf_op | source)
XLA Modules:
  0.0 117.0 jit_solution(9591740409893140895)
XLA Ops:
  0.6 0.0 copy-start
  0.6 1.0 copy-done
  1.6 0.0 copy-start.1
  1.6 0.9 copy-done.1
  2.6 0.0 copy-start.2
  2.6 0.7 copy-done.2
  3.2 0.0 copy-start.3
  3.2 0.7 copy-done.3
  3.9 110.0 %layer.1 = (bf16[128,1536]{1,0:T(8,128)(2,1)S(1)}, f32[8,128]{1,0:T(8,128)S(1)}, bf16[192,512]{1,0:T(8,128)(2,1)S(1)}, bf16[512,1536]{1,0:T(8,128)(2,1)S(1)}) custom-call(s32[2,128]{1,0:T(2,128)S(1)} %bitcast.11, f32[2,128]{1,0:T(2,128)S(1)} %bitcast.12, bf16[192,512]{1,0:T(8,128)(2,1)S(1)} %bitcast.9, bf16[512,1536]{1,0:T(8,128)(2,1)} %bitcast.13, ...), custom_call_target="tpu_custom_call" | custom-call | tf_op jit(solution)/shard_map/layer/pallas_call | solution.py:342
  113.9 0.6 slice_bitcast_fusion
  114.5 0.7 copy.12
  115.2 0.7 copy.13
  115.9 1.1 copy.14
Async XLA Ops:
  0.6 1.0 copy-start
  1.6 0.9 copy-start.1
  2.6 0.7 copy-start.2
  3.2 0.7 copy-start.3

commit v2 on v1

--- a/solution.py
+++ b/solution.py
@@ -13,20 +13,24 @@
 
 NX, NY, NE = 4, 4, 8
 CAP, ROWS, DEPTH, COLS, TOKS = 48, 192, 512, 1536, 128
-GROUPS = 3
+GROUPS = 6
 WIDE = COLS // GROUPS
 LANES = 128
 CHUNKS = COLS // LANES
 PER_GROUP = WIDE // LANES
-STEPS = CHUNKS + NE - 1
+HOP = 3
+STEPS = CHUNKS + HOP * (NE - 1)
+FORWARD_AT, HGRAD_AT = 10, 16
+WGRAD_AT = HGRAD_AT + NX
 
 
 def kernel(
-    ids_ref, gates_ref, hidden_ref, weight_ref, cot_ref,
+    ids_in, gates_in, hidden_in, weight_in, cot_in,
     mixed_ref, gate_ref, hgrad_ref, wgrad_ref,
-    hid_all, slot_all, cot_sel, parts, core_rx, core_sum, y_rx, z_own, z_tx, z_rx,
+    ids_ref, gates_ref, weight_ref, cot_ref,
+    hid_all, hid_t, slot_all, cot_sel, parts, core_rx, core_sum, y_rx, z_own, z_tx, z_rx,
     tok, up_tx, up_rx, down_tx, down_rx, hg_tx, hg_rx, gate_tx, gate_sum, gate_xrx, gate_erx, gate_acc,
-    hid_sem, slot_z_sem, slot_y_sem, slot_c_sem, core_sem, y_sem, z_sem, up_sem, down_sem, hg_sem, gx_sem, ge_sem,
+    in_sem, hid_sem, slot_z_sem, slot_y_sem, slot_c_sem, core_sem, y_sem, z_sem, up_sem, down_sem, hg_sem, gx_sem, ge_sem,
 ):
     dp = lax.axis_index("dp")
     ex = lax.axis_index("expert")
@@ -66,6 +70,30 @@
     for peer in peers:
         pl.semaphore_signal(barrier, inc=1, device_id=peer, device_id_type=MESH)
 
+    def fetch(src, dst, index):
+        return pltpu.make_async_copy(src, dst, in_sem.at[index])
+
+    fetches = [
+        fetch(ids_in, ids_ref, 0),
+        fetch(gates_in, gates_ref, 1),
+        fetch(hidden_in, hid_all.at[mx], 2),
+        fetch(cot_in, cot_ref, 3),
+        fetch(weight_in, weight_ref, 4),
+    ]
+    for copy in fetches:
+        copy.start()
+
+    fetches[2].wait()
+    pl.semaphore_wait(barrier, len(peers))
+
+    hid_copies = [
+        remote(hid_all.at[mx], hid_all.at[mx], hid_sem, (d - 1,), x_peer(d)) for d in (1, 3, 2)
+    ]
+    for copy in hid_copies:
+        copy.start()
+
+    fetches[0].wait()
+    fetches[1].wait()
     hit0 = (ids_ref[0:1, :] == ex).astype(F32)
     hit1 = (ids_ref[1:2, :] == ex).astype(F32)
     hits = hit0 + hit1
@@ -82,19 +110,12 @@
     sel = jnp.where(slot == place, jnp.broadcast_to(hits, (CAP, TOKS)), 0.0)
     slot_gate = jnp.sum(sel * gate_of, axis=1, keepdims=True)
     sel16 = sel.astype(BF16)
+    fetches[3].wait()
     picked = jnp.dot(sel16, cot_ref[...], preferred_element_type=F32)
-    cot_sel[...] = picked
+    for g in range(GROUPS):
+        cot_sel[g] = picked[:, g * WIDE : (g + 1) * WIDE]
     slot_all[dp] = (slot_gate * picked).astype(BF16)
-    hid_all[mx] = hidden_ref[...]
     gate_acc[...] = jnp.zeros_like(gate_acc)
-
-    pl.semaphore_wait(barrier, len(peers))
-
-    hid_copies = [
-        remote(hidden_ref, hid_all.at[mx], hid_sem, (d - 1,), x_peer(d)) for d in (1, 3, 2)
-    ]
-    for copy in hid_copies:
-        copy.start()
 
     def slot_y(side, block):
         return [
@@ -114,33 +135,44 @@
     core_copies = [slot_core(0, dp)]
     core_copies[0].start()
 
-    for copy in hid_copies:
-        copy.wait_recv()
-    rows_all = hid_all[...].reshape(NX * ROWS, DEPTH)
-    to_core = []
-    for g in range(GROUPS):
-        product = jnp.dot(
-            rows_all, weight_ref[:, g * WIDE : (g + 1) * WIDE], preferred_element_type=F32
-        ).astype(BF16)
-        product = product.reshape(NY, 2, 2, CAP, WIDE)
-        for c in range(2):
-            parts[g, c] = product[:, :, c]
-        copy = remote(parts.at[g, 1 - core], core_rx.at[g], core_sem, (g,), core_peer)
-        copy.start()
-        to_core.append(copy)
-
-    to_y = []
-    for g in range(GROUPS):
-        to_core[g].wait_recv()
-        core_sum[g] = (parts[g, core].astype(F32) + core_rx[g].astype(F32)).astype(BF16)
-        group = []
-        for d in (2, 1, 3):
-            copy = remote(
-                core_sum.at[g, (row + d) % NY], y_rx.at[g, d - 1], y_sem, (g, d - 1), y_peer(d)
-            )
-            copy.start()
-            group.append(copy)
-        to_y.append(group)
+    fetches[4].wait()
+
+    def core_copy(block, g):
+        return remote(
+            parts.at[block, g, 1 - core], core_rx.at[block, g], core_sem, (block, g), core_peer
+        )
+
+    def row_copy(d, g):
+        return remote(
+            core_sum.at[(row + d) % NY, g], y_rx.at[g, d - 1], y_sem, (g, d - 1), y_peer(d)
+        )
+
+    to_z = []
+    for copy, d in [(None, 0), *zip(hid_copies, (1, 3, 2))]:
+        block = (mx - d + NX) % NX
+        if copy is not None:
+            copy.wait_recv()
+        for g in range(GROUPS):
+            product = jnp.dot(
+                hid_all[block],
+                weight_ref[:, g * WIDE : (g + 1) * WIDE],
+                preferred_element_type=F32,
+            ).astype(BF16)
+            product = product.reshape(2, 2, CAP, WIDE)
+            for c in range(2):
+                parts[block, g, c] = product[:, c]
+            core_copy(block, g).start()
+        away = (block - row + NY) % NY
+        for g in range(GROUPS):
+            core_copy(block, g).wait_recv()
+            core_sum[block, g] = (
+                parts[block, g, core].astype(F32) + core_rx[block, g].astype(F32)
+            ).astype(BF16)
+
+            @pl.when(away > 0)
+            def _():
+                row_copy(away, g).start()
+
 
     for n, copy in enumerate(own_y):
         copy.wait_recv()
@@ -148,19 +180,13 @@
         onward = slot_core(1 + n, dp_of((row - d + NY) % NY, half, core))
         onward.start()
         core_copies.append(onward)
-    slot_z.wait_recv()
+    hid_t[...] = hid_all[...].reshape(NX * ROWS, DEPTH).T
     other_y = slot_y(1, other_block)
-    for copy in other_y:
-        copy.start()
-    onward = slot_core(4, other_block)
-    onward.start()
-    core_copies.append(onward)
-
-    to_z = []
+
     for g in range(GROUPS):
-        for copy in to_y[g]:
-            copy.wait_recv()
-        mine = core_sum[g, row].astype(F32)
+        for d in range(1, NY):
+            row_copy(d, g).wait_recv()
+        mine = core_sum[row, g].astype(F32)
         for d in range(1, NY):
             mine = mine + y_rx[g, d - 1].astype(F32)
         z_own[g] = mine
@@ -168,48 +194,25 @@
         copy = remote(z_tx.at[g], z_rx.at[g], z_sem, (g,), half_peer)
         copy.start()
         to_z.append(copy)
-
-    for n, copy in enumerate(other_y):
-        copy.wait_recv()
-        d = (1, 3, 2)[n]
-        onward = slot_core(5 + n, dp_of((row - d + NY) % NY, 1 - half, core))
-        onward.start()
-        core_copies.append(onward)
-    for copy in core_copies:
-        copy.wait_recv()
-
-    slots = slot_all[...].reshape(NX * ROWS, COLS)
-    hg_tx[...] = (
-        lax.dot_general(slots, weight_ref[...], NT, preferred_element_type=F32)
-        .astype(BF16)
-        .reshape(NX, ROWS, DEPTH)
-    )
-    hg_copies = [
-        remote(hg_tx.at[(mx + d) % NX], hg_rx.at[d - 1], hg_sem, (d - 1,), x_peer(d))
-        for d in (2, 1, 3)
+        if g == GROUPS // 2:
+            slot_z.wait_recv()
+            for copy in other_y:
+                copy.start()
+            onward = slot_core(4, other_block)
+            onward.start()
+            core_copies.append(onward)
+    onwards = [
+        slot_core(5 + n, dp_of((row - d + NY) % NY, 1 - half, core))
+        for n, d in enumerate((1, 3, 2))
     ]
-    for copy in hg_copies:
-        copy.start()
-    rows_t = hid_all[...].reshape(NX * ROWS, DEPTH).T
-    for g in range(GROUPS):
-        wgrad_ref[:, g * WIDE : (g + 1) * WIDE] = jnp.dot(
-            rows_t,
-            slot_all[:, :, g * WIDE : (g + 1) * WIDE].reshape(NX * ROWS, WIDE),
-            preferred_element_type=F32,
-        ).astype(BF16)
+    core_copies += onwards
 
     sel_t = sel.T.astype(BF16)
 
     def take_group(g):
         remote(z_tx.at[g], z_rx.at[g], z_sem, (g,), half_peer).wait_recv()
         out = (z_own[g, half] + z_rx[g].astype(F32)).astype(BF16).astype(F32)
-        for n in range(GROUPS):
-
-            @pl.when(g == n)
-            def _():
-                dots = out * cot_sel[:, n * WIDE : (n + 1) * WIDE]
-                gate_acc[...] += jnp.sum(dots, axis=1, keepdims=True)
-
+        gate_acc[...] += jnp.sum(out * cot_sel[g], axis=1, keepdims=True)
         weighted = jnp.dot(
             sel_t, (slot_gate * out).astype(BF16), preferred_element_type=F32
         ).astype(BF16)
@@ -227,6 +230,10 @@
     gate_x = [remote(gate_tx, gate_xrx.at[d - 1], gx_sem, (d - 1,), x_peer(d)) for d in (2, 1, 3)]
     gate_e = [
         remote(gate_sum, gate_erx.at[d - 1], ge_sem, (d - 1,), e_peer(d)) for d in range(1, NE)
+    ]
+    hg_copies = [
+        remote(hg_tx.at[(mx + d) % NX], hg_rx.at[d - 1], hg_sem, (d - 1,), x_peer(d))
+        for d in (2, 1, 3)
     ]
 
     def step(s, carry):
@@ -243,7 +250,7 @@
             for copy in gate_x:
                 copy.start()
 
-        @pl.when(s == CHUNKS + 2)
+        @pl.when(s == CHUNKS + 3)
         def _():
             for copy in gate_x:
                 copy.wait_recv()
@@ -251,7 +258,7 @@
             for copy in gate_e:
                 copy.start()
 
-        q = s - ex
+        q = s - HOP * ex
 
         @pl.when(jnp.logical_and(q >= 0, q < CHUNKS))
         def _():
@@ -268,7 +275,7 @@
             def _():
                 up_copy(q).start()
 
-        r = s - (NE - 1 - ex)
+        r = s - HOP * (NE - 1 - ex)
 
         @pl.when(jnp.logical_and(r >= 0, r < CHUNKS))
         def _():
@@ -284,6 +291,40 @@
             @pl.when(ex > 0)
             def _():
                 down_copy(r).start()
+
+        @pl.when(s == FORWARD_AT)
+        def _():
+            for copy, onward in zip(other_y, onwards):
+                copy.wait_recv()
+                onward.start()
+
+        @pl.when(s == HGRAD_AT)
+        def _():
+            for copy in core_copies:
+                copy.wait_recv()
+
+        for n, d in enumerate((2, 1, 3, 0)):
+
+            @pl.when(s == HGRAD_AT + n)
+            def _():
+                block = (mx + d) % NX
+                slots = slot_all[pl.ds(block * 4, 4)].reshape(ROWS, COLS)
+                hg_tx[block] = lax.dot_general(
+                    slots, weight_ref[...], NT, preferred_element_type=F32
+                ).astype(BF16)
+                if d:
+                    hg_copies[n].start()
+
+        for g in range(GROUPS):
+
+            @pl.when(s == WGRAD_AT + g)
+            def _():
+                columns = slice(g * WIDE, (g + 1) * WIDE)
+                wgrad_ref[:, columns] = jnp.dot(
+                    hid_t[...],
+                    slot_all[:, :, columns].reshape(NX * ROWS, WIDE),
+                    preferred_element_type=F32,
+                ).astype(BF16)
 
         return carry
 
@@ -312,13 +353,15 @@
     gates = gate_sum[...]
     for d in range(1, NE):
         gates = gates + gate_erx[d - 1]
-    gate_ref[...] = gates
-
-    for copy in [*hid_copies, slot_z, *own_y, *other_y, *core_copies, *to_core, *to_z]:
+    gate_ref[...] = gates[0:2, :]
+
+    for copy in [*hid_copies, slot_z, *own_y, *other_y, *core_copies, *to_z]:
         copy.wait_send()
-    for group in to_y:
-        for copy in group:
-            copy.wait_send()
+    for g in range(GROUPS):
+        for block in range(NY):
+            core_copy(block, g).wait_send()
+        for d in range(1, NY):
+            row_copy(d, g).wait_send()
     for copy in [*hg_copies, *gate_x, *gate_e]:
         copy.wait_send()
 
@@ -338,25 +381,34 @@
 
 def body(expert_ids, gate_weights, hidden, down_weight, cotangent):
     vmem = pl.BlockSpec(memory_space=pltpu.VMEM)
+    hbm = pl.BlockSpec(memory_space=pltpu.HBM)
     dma = pltpu.SemaphoreType.DMA
+    shapes = (
+        jax.ShapeDtypeStruct((TOKS, COLS), BF16),
+        jax.ShapeDtypeStruct((2, TOKS), F32),
+        jax.ShapeDtypeStruct((ROWS, DEPTH), BF16),
+        jax.ShapeDtypeStruct((DEPTH, COLS), BF16),
+    )
+    operands = (expert_ids.T, gate_weights.T, hidden[0], down_weight[0], cotangent)
+    operands = [pltpu.with_memory_space_constraint(each, pltpu.HBM) for each in operands]
     mixed, gates, hgrad, wgrad = pl.pallas_call(
         kernel,
         name="layer",
-        out_shape=(
-            jax.ShapeDtypeStruct((TOKS, COLS), BF16),
-            jax.ShapeDtypeStruct((8, TOKS), F32),
-            jax.ShapeDtypeStruct((ROWS, DEPTH), BF16),
-            jax.ShapeDtypeStruct((DEPTH, COLS), BF16),
-        ),
-        in_specs=[vmem] * 5,
+        out_shape=shapes,
+        in_specs=[hbm] * 5,
         out_specs=(vmem,) * 4,
         scratch_shapes=[
+            pltpu.VMEM((2, TOKS), jnp.int32),
+            pltpu.VMEM((2, TOKS), F32),
+            pltpu.VMEM((DEPTH, COLS), BF16),
+            pltpu.VMEM((TOKS, COLS), BF16),
             pltpu.VMEM((NX, ROWS, DEPTH), BF16),
+            pltpu.VMEM((DEPTH, NX * ROWS), BF16),
             pltpu.VMEM((16, CAP, COLS), BF16),
-            pltpu.VMEM((CAP, COLS), F32),
-            pltpu.VMEM((GROUPS, 2, NY, 2, CAP, WIDE), BF16),
-            pltpu.VMEM((GROUPS, NY, 2, CAP, WIDE), BF16),
-            pltpu.VMEM((GROUPS, NY, 2, CAP, WIDE), BF16),
+            pltpu.VMEM((GROUPS, CAP, WIDE), F32),
+            pltpu.VMEM((NY, GROUPS, 2, 2, CAP, WIDE), BF16),
+            pltpu.VMEM((NY, GROUPS, 2, CAP, WIDE), BF16),
+            pltpu.VMEM((NY, GROUPS, 2, CAP, WIDE), BF16),
             pltpu.VMEM((GROUPS, NY - 1, 2, CAP, WIDE), BF16),
             pltpu.VMEM((GROUPS, 2, CAP, WIDE), F32),
             pltpu.VMEM((GROUPS, CAP, WIDE), BF16),
@@ -373,11 +425,12 @@
             pltpu.VMEM((NX - 1, 8, TOKS), F32),
             pltpu.VMEM((NE - 1, 8, TOKS), F32),
             pltpu.VMEM((CAP, TOKS), F32),
+            dma((5,)),
             dma((2, NX - 1)),
             dma((2, 1)),
             dma((2, 2, NY - 1)),
             dma((2, 8)),
-            dma((2, GROUPS)),
+            dma((2, NY, GROUPS)),
             dma((2, GROUPS, NY - 1)),
             dma((2, GROUPS)),
             dma((2, CHUNKS)),
@@ -389,8 +442,8 @@
         compiler_params=pltpu.CompilerParams(
             collective_id=0, has_side_effects=True, vmem_limit_bytes=50 * 2**20
         ),
-    )(expert_ids.T, gate_weights.T, hidden[0], down_weight[0], cotangent)
-    return mixed, gates[0:2].T, hgrad[None], wgrad[None]
+    )(*operands)
+    return mixed, gates.T, hgrad[None], wgrad[None]
 
 
 def solution(mesh):

time: 118 us -> 90 us (0.76)
  the two profiles are of different devices: /device:TPU:6 before, /device:TPU:4 now
where the time goes in v2:
time: 90 us; the launch traced here: 89.9 us
  Pallas kernels  86.1 us (96%)
  local copies, waits for them, and re-layouts  3.13 us (3%)
    pallas_call x1, Pallas kernels, body(): pl.pallas_call(kernel, name='layer', out_shape=shapes, in_specs=[hbm] * 5...  86.1 us
    unnamed x4, local copies, waits for them, and re-layouts  3.13 us

profile of v2, /device:TPU:4, one launch (start us, length us, event | category | flops | bytes accessed | tf_op | source)
XLA Modules:
  0.0 89.9 jit_solution(5250694734162505220)
XLA Ops:
  0.6 86.1 %layer.1 = (bf16[128,1536]{1,0:T(8,128)(2,1)S(1)}, f32[2,128]{1,0:T(2,128)S(1)}, bf16[192,512]{1,0:T(8,128)(2,1)S(1)}, bf16[512,1536]{1,0:T(8,128)(2,1)S(1)}) custom-call(s32[2,128]{1,0:T(2,128)} %bitcast.12, f32[2,128]{1,0:T(2,128)} %bitcast.13, bf16[192,512]{1,0:T(8,128)(2,1)} %bitcast.11, bf16[512,1536]{1,0:T(8,128)(2,1)} %bitcast.10, ...), custom_call_target="tpu_custom_call" | custom-call | tf_op jit(solution)/shard_map/layer/pallas_call | solution.py:394
  86.8 0.7 copy.13
  87.5 0.6 copy.14
  88.1 0.7 copy.15
  88.8 1.1 %copy.16 = bf16[1,512,1536]{2,1,0:T(8,128)(2,1)} copy(bf16[1,512,1536]{2,1,0:T(8,128)(2,1)S(1)} %bitcast.7) | data formatting | bytes 3145728

commit v3 on v2

--- a/solution.py
+++ b/solution.py
@@ -18,7 +18,7 @@
 LANES = 128
 CHUNKS = COLS // LANES
 PER_GROUP = WIDE // LANES
-HOP = 3
+HOP = 5
 STEPS = CHUNKS + HOP * (NE - 1)
 FORWARD_AT, HGRAD_AT = 10, 16
 WGRAD_AT = HGRAD_AT + NX
@@ -137,41 +137,33 @@
 
     fetches[4].wait()
 
-    def core_copy(block, g):
-        return remote(
-            parts.at[block, g, 1 - core], core_rx.at[block, g], core_sem, (block, g), core_peer
-        )
+    def core_copy(g):
+        return remote(parts.at[g, 1 - core], core_rx.at[g], core_sem, (g,), core_peer)
 
     def row_copy(d, g):
         return remote(
-            core_sum.at[(row + d) % NY, g], y_rx.at[g, d - 1], y_sem, (g, d - 1), y_peer(d)
+            core_sum.at[g, (row + d) % NY], y_rx.at[g, d - 1], y_sem, (g, d - 1), y_peer(d)
         )
 
     to_z = []
-    for copy, d in [(None, 0), *zip(hid_copies, (1, 3, 2))]:
-        block = (mx - d + NX) % NX
-        if copy is not None:
-            copy.wait_recv()
-        for g in range(GROUPS):
+    for copy in hid_copies:
+        copy.wait_recv()
+    rows_all = hid_all[...].reshape(NX * ROWS, DEPTH)
+    for g in range(GROUPS + 2):
+        if g < GROUPS:
             product = jnp.dot(
-                hid_all[block],
-                weight_ref[:, g * WIDE : (g + 1) * WIDE],
-                preferred_element_type=F32,
+                rows_all, weight_ref[:, g * WIDE : (g + 1) * WIDE], preferred_element_type=F32
             ).astype(BF16)
-            product = product.reshape(2, 2, CAP, WIDE)
+            product = product.reshape(NY, 2, 2, CAP, WIDE)
             for c in range(2):
-                parts[block, g, c] = product[:, c]
-            core_copy(block, g).start()
-        away = (block - row + NY) % NY
-        for g in range(GROUPS):
-            core_copy(block, g).wait_recv()
-            core_sum[block, g] = (
-                parts[block, g, core].astype(F32) + core_rx[block, g].astype(F32)
-            ).astype(BF16)
-
-            @pl.when(away > 0)
-            def _():
-                row_copy(away, g).start()
+                parts[g, c] = product[:, :, c]
+            core_copy(g).start()
+        if g >= 2:
+            n = g - 2
+            core_copy(n).wait_recv()
+            core_sum[n] = (parts[n, core].astype(F32) + core_rx[n].astype(F32)).astype(BF16)
+            for d in (2, 1, 3):
+                row_copy(d, n).start()
 
 
     for n, copy in enumerate(own_y):
@@ -186,7 +178,7 @@
     for g in range(GROUPS):
         for d in range(1, NY):
             row_copy(d, g).wait_recv()
-        mine = core_sum[row, g].astype(F32)
+        mine = core_sum[g, row].astype(F32)
         for d in range(1, NY):
             mine = mine + y_rx[g, d - 1].astype(F32)
         z_own[g] = mine
@@ -358,8 +350,7 @@
     for copy in [*hid_copies, slot_z, *own_y, *other_y, *core_copies, *to_z]:
         copy.wait_send()
     for g in range(GROUPS):
-        for block in range(NY):
-            core_copy(block, g).wait_send()
+        core_copy(g).wait_send()
         for d in range(1, NY):
             row_copy(d, g).wait_send()
     for copy in [*hg_copies, *gate_x, *gate_e]:
@@ -377,6 +368,17 @@
         return carry
 
     lax.fori_loop(0, CHUNKS, drain, 0)
+
+
+def write_out(*refs):
+    count = (len(refs) - 1) // 2
+    copies = [
+        pltpu.make_async_copy(refs[n], refs[count + n], refs[-1].at[n]) for n in range(count)
+    ]
+    for copy in copies:
+        copy.start()
+    for copy in copies:
+        copy.wait()
 
 
 def body(expert_ids, gate_weights, hidden, down_weight, cotangent):
@@ -391,7 +393,7 @@
     )
     operands = (expert_ids.T, gate_weights.T, hidden[0], down_weight[0], cotangent)
     operands = [pltpu.with_memory_space_constraint(each, pltpu.HBM) for each in operands]
-    mixed, gates, hgrad, wgrad = pl.pallas_call(
+    results = pl.pallas_call(
         kernel,
         name="layer",
         out_shape=shapes,
@@ -406,9 +408,9 @@
             pltpu.VMEM((DEPTH, NX * ROWS), BF16),
             pltpu.VMEM((16, CAP, COLS), BF16),
             pltpu.VMEM((GROUPS, CAP, WIDE), F32),
-            pltpu.VMEM((NY, GROUPS, 2, 2, CAP, WIDE), BF16),
-            pltpu.VMEM((NY, GROUPS, 2, CAP, WIDE), BF16),
-            pltpu.VMEM((NY, GROUPS, 2, CAP, WIDE), BF16),
+            pltpu.VMEM((GROUPS, 2, NY, 2, CAP, WIDE), BF16),
+            pltpu.VMEM((GROUPS, NY, 2, CAP, WIDE), BF16),
+            pltpu.VMEM((GROUPS, NY, 2, CAP, WIDE), BF16),
             pltpu.VMEM((GROUPS, NY - 1, 2, CAP, WIDE), BF16),
             pltpu.VMEM((GROUPS, 2, CAP, WIDE), F32),
             pltpu.VMEM((GROUPS, CAP, WIDE), BF16),
@@ -430,7 +432,7 @@
             dma((2, 1)),
             dma((2, 2, NY - 1)),
             dma((2, 8)),
-            dma((2, NY, GROUPS)),
+            dma((2, GROUPS)),
             dma((2, GROUPS, NY - 1)),
             dma((2, GROUPS)),
             dma((2, CHUNKS)),
@@ -443,6 +445,15 @@
             collective_id=0, has_side_effects=True, vmem_limit_bytes=50 * 2**20
         ),
     )(*operands)
+    results = [pltpu.with_memory_space_constraint(each, pltpu.VMEM) for each in results]
+    mixed, gates, hgrad, wgrad = pl.pallas_call(
+        write_out,
+        name="write_out",
+        out_shape=shapes,
+        in_specs=[vmem] * 4,
+        out_specs=(hbm,) * 4,
+        scratch_shapes=[dma((4,))],
+    )(*results)
     return mixed, gates.T, hgrad[None], wgrad[None]
 
 

time: 90 us -> 82.2 us (0.913)
  the two profiles are of different devices: /device:TPU:4 before, /device:TPU:6 now
where the time goes in v3:
time: 82.2 us; the launch traced here: 81.5 us
  Pallas kernels  80.9 us (98%)
    pallas_call x1, Pallas kernels, body(): pl.pallas_call(kernel, name='layer', out_shape=shapes, in_specs=[hbm] * 5...  79.5 us

profile of v3, /device:TPU:6, one launch (start us, length us, event | category | flops | bytes accessed | tf_op | source)
XLA Modules:
  0.0 81.5 jit_solution(6367980582219710830)
XLA Ops:
  0.6 79.5 %layer.1 = (bf16[128,1536]{1,0:T(8,128)(2,1)S(1)}, f32[2,128]{1,0:T(2,128)S(1)}, bf16[192,512]{1,0:T(8,128)(2,1)S(1)}, bf16[512,1536]{1,0:T(8,128)(2,1)S(1)}) custom-call(s32[2,128]{1,0:T(2,128)} %bitcast.9, f32[2,128]{1,0:T(2,128)} %bitcast.10, bf16[192,512]{1,0:T(8,128)(2,1)} %bitcast.8, bf16[512,1536]{1,0:T(8,128)(2,1)} %bitcast.7, bf16[128,1536]{1,0:T(8,128)(2,1)} %cot_in.1), custom_call_target="tpu_custom_call" | custom-call | tf_op jit(solution)/shard_map/layer/pallas_call | solution.py:396
  80.1 1.4 %write_out.1 = (bf16[128,1536]{1,0:T(8,128)(2,1)}, f32[2,128]{1,0:T(2,128)}, bf16[192,512]{1,0:T(8,128)(2,1)}, bf16[512,1536]{1,0:T(8,128)(2,1)}) custom-call(bf16[128,1536]{1,0:T(8,128)(2,1)S(1)} %get-tuple-element.12.refs_0_, f32[2,128]{1,0:T(2,128)S(1)} %get-tuple-element.13.refs_1_, bf16[192,512]{1,0:T(8,128)(2,1)S(1)} %get-tuple-element.14.refs_2_, ...), custom_call_target="tpu_custom_call" | custom-call | tf_op jit(solution)/shard_map/write_out/pallas_call | solution.py:449

commit v4 on v3

--- a/solution.py
+++ b/solution.py
@@ -13,6 +13,7 @@
 
 NX, NY, NE = 4, 4, 8
 CAP, ROWS, DEPTH, COLS, TOKS = 48, 192, 512, 1536, 128
+HALF_ROWS = ROWS // 2
 GROUPS = 6
 WIDE = COLS // GROUPS
 LANES = 128
@@ -86,8 +87,20 @@
     fetches[2].wait()
     pl.semaphore_wait(barrier, len(peers))
 
+    def hid_copy(index, block, part, d):
+        ref = hid_all.at[block, pl.ds(part * HALF_ROWS, HALF_ROWS)]
+        return remote(ref, ref, hid_sem, (index,), x_peer(d))
+
+    right, left = 1, NX - 1
     hid_copies = [
-        remote(hid_all.at[mx], hid_all.at[mx], hid_sem, (d - 1,), x_peer(d)) for d in (1, 3, 2)
+        hid_copy(0, mx, 0, right),
+        hid_copy(1, mx, 1, left),
+        hid_copy(2, mx, 1, right),
+        hid_copy(3, mx, 0, left),
+    ]
+    hid_onward = [
+        hid_copy(4, (mx + left) % NX, 0, right),
+        hid_copy(5, (mx + right) % NX, 1, left),
     ]
     for copy in hid_copies:
         copy.start()
@@ -134,6 +147,9 @@
         copy.start()
     core_copies = [slot_core(0, dp)]
     core_copies[0].start()
+    for copy, onward in zip(hid_copies, hid_onward):
+        copy.wait_recv()
+        onward.start()
 
     fetches[4].wait()
 
@@ -146,7 +162,7 @@
         )
 
     to_z = []
-    for copy in hid_copies:
+    for copy in [*hid_copies[2:], *hid_onward]:
         copy.wait_recv()
     rows_all = hid_all[...].reshape(NX * ROWS, DEPTH)
     for g in range(GROUPS + 2):
@@ -162,7 +178,7 @@
             n = g - 2
             core_copy(n).wait_recv()
             core_sum[n] = (parts[n, core].astype(F32) + core_rx[n].astype(F32)).astype(BF16)
-            for d in (2, 1, 3):
+            for d in (1, 3, 2):
                 row_copy(d, n).start()
 
 
@@ -347,7 +363,7 @@
         gates = gates + gate_erx[d - 1]
     gate_ref[...] = gates[0:2, :]
 
-    for copy in [*hid_copies, slot_z, *own_y, *other_y, *core_copies, *to_z]:
+    for copy in [*hid_copies, *hid_onward, slot_z, *own_y, *other_y, *core_copies, *to_z]:
         copy.wait_send()
     for g in range(GROUPS):
         core_copy(g).wait_send()
@@ -428,7 +444,7 @@
             pltpu.VMEM((NE - 1, 8, TOKS), F32),
             pltpu.VMEM((CAP, TOKS), F32),
             dma((5,)),
-            dma((2, NX - 1)),
+            dma((2, 6)),
             dma((2, 1)),
             dma((2, 2, NY - 1)),
             dma((2, 8)),

time: 82.2 us -> 80.4 us (0.978)
  Pallas kernels: 80.9 us -> 79.6 us
    pallas_call x1, Pallas kernels: 79.5 us -> 78.2 us  [body(): pl.pallas_call(kernel, name='layer', out_shape=shapes, in_specs=[hbm] * 5...]
where the time goes in v4:
time: 80.4 us; the launch traced here: 80.2 us
  Pallas kernels  79.6 us (99%)
    pallas_call x1, Pallas kernels, body(): pl.pallas_call(kernel, name='layer', out_shape=shapes, in_specs=[hbm] * 5...  78.2 us

profile of v4, /device:TPU:6, one launch (start us, length us, event | category | flops | bytes accessed | tf_op | source)
XLA Modules:
  0.0 80.2 jit_solution(17070045823941138796)
XLA Ops:
  0.6 78.2 %layer.1 = (bf16[128,1536]{1,0:T(8,128)(2,1)S(1)}, f32[2,128]{1,0:T(2,128)S(1)}, bf16[192,512]{1,0:T(8,128)(2,1)S(1)}, bf16[512,1536]{1,0:T(8,128)(2,1)S(1)}) custom-call(s32[2,128]{1,0:T(2,128)} %bitcast.9, f32[2,128]{1,0:T(2,128)} %bitcast.10, bf16[192,512]{1,0:T(8,128)(2,1)} %bitcast.8, bf16[512,1536]{1,0:T(8,128)(2,1)} %bitcast.7, bf16[128,1536]{1,0:T(8,128)(2,1)} %cot_in.1), custom_call_target="tpu_custom_call" | custom-call | tf_op jit(solution)/shard_map/layer/pallas_call | solution.py:412
  78.8 1.4 %write_out.1 = (bf16[128,1536]{1,0:T(8,128)(2,1)}, f32[2,128]{1,0:T(2,128)}, bf16[192,512]{1,0:T(8,128)(2,1)}, bf16[512,1536]{1,0:T(8,128)(2,1)}) custom-call(bf16[128,1536]{1,0:T(8,128)(2,1)S(1)} %get-tuple-element.12.refs_0_, f32[2,128]{1,0:T(2,128)S(1)} %get-tuple-element.13.refs_1_, bf16[192,512]{1,0:T(8,128)(2,1)S(1)} %get-tuple-element.14.refs_2_, ...), custom_call_target="tpu_custom_call" | custom-call | tf_op jit(solution)/shard_map/write_out/pallas_call | solution.py:465
